TPU v7x, 32 devices: a whole 2x2x4 slice. The times are simulated.
32 devices in a mesh: grp: 2 (over x), tm: 16 (over z, y, core).
Axes of the slice: x: 2, y: 2, z: 4, core: 2. Of those that a mesh axis runs over, the one named last changes fastest.
Arguments:
- series: bfloat16 [32768, 4096], P('grp', 'tm'), parts along dimension 0, may hold values from -8 to 8
- start_block: bfloat16 [32, 16384], replicated, may hold values from -6 to 6
Outputs:
- basis: float32 [32, 32768], P(None, ('grp', 'tm')), parts along dimension 1
- projected: float32 [32, 8192], P(None, ('grp', 'tm')), parts along dimension 1
There are 2 independent parts, one for each index of `grp`. A program takes and returns all parts, laid end to end along the dimension named above; an argument that names none is the same for every part. Nothing has to cross between parts.
All inputs are finite; a program needn't handle non-finite values.
Results may differ from a plain program's by a relative error of at most 0.002.
The roundings to bfloat16 on the way count: a program that leaves them out, or rounds other values in their place, can miss the bound.
Values may be sent and summed in bfloat16 or wider, within the bound.
A program may use at most 128 MiB of HBM per device.

v0:
```python
import jax
import jax.numpy as jnp
from jax import lax
from jax.sharding import PartitionSpec as P

ITERS = 2


THRESH = 1.0


def prefix_2(part, axis, combine, identity):
    place = lax.axis_index(axis)
    gathered = lax.all_gather(part, axis)
    state = jnp.zeros_like(part) + jnp.asarray(identity, part.dtype)

    def one(hop, state):
        return combine(state, lax.dynamic_index_in_dim(gathered, hop, 0, False))

    return lax.fori_loop(0, place, one, state)


def add_terms(earlier, later):
    return earlier + later


def shifted(gram):
    width = gram.shape[0]
    amount = 1e-05 * jnp.trace(gram) / width + 1e-06
    return gram + amount * jnp.eye(width, dtype=gram.dtype)


def body(series, start_block):
    series_count, blocks = series.shape
    count = lax.axis_size("tm")
    place = lax.axis_index("tm")
    row_id = lax.broadcasted_iota(jnp.int32, (blocks, blocks), 0)
    col_id = lax.broadcasted_iota(jnp.int32, (blocks, blocks), 1)
    triangle = (row_id <= col_id).astype(jnp.bfloat16)
    partial_sums = jnp.dot(series, triangle, preferred_element_type=jnp.float32)
    own_total = partial_sums[:, -1]
    before = prefix_2(own_total, "tm", add_terms, jnp.zeros_like(own_total))
    total = lax.psum(own_total, "tm")
    prefix = partial_sums + before[:, None]
    steps_f = jnp.float32(blocks * count)
    t_local = (place * blocks + jnp.arange(1, blocks + 1, dtype=jnp.int32)).astype(jnp.float32)
    weight = jnp.where(
        t_local < steps_f, jnp.sqrt(steps_f / jnp.maximum(t_local * (steps_f - t_local), 1.0)), 0.0
    )
    frac = t_local / steps_f
    raw = weight[None, :] * (prefix - frac[None, :] * total[:, None])
    cusum = raw.astype(jnp.bfloat16)
    sparse = (jnp.sign(raw) * jnp.maximum(jnp.abs(raw) - THRESH, 0.0)).astype(jnp.bfloat16)
    share_rows = series_count // count
    block = start_block
    basis_share = jnp.zeros((start_block.shape[0], share_rows), jnp.float32)
    for step in range(ITERS):
        scores = jnp.dot(block, sparse, preferred_element_type=jnp.float32).astype(jnp.bfloat16)
        local_image = lax.dot_general(
            scores, sparse, (((1,), (1,)), ((), ())), preferred_element_type=jnp.float32
        )
        image = lax.psum(local_image, "tm")
        gram = jnp.dot(image, image.T, precision=lax.Precision.HIGHEST)
        lower = jnp.linalg.cholesky(shifted(gram))
        first = jax.scipy.linalg.solve_triangular(lower, image, lower=True)
        gram_next = jnp.dot(first, first.T, precision=lax.Precision.HIGHEST)
        lower_next = jnp.linalg.cholesky(shifted(gram_next))
        basis_full = jax.scipy.linalg.solve_triangular(lower_next, first, lower=True)
        basis_share = lax.dynamic_slice_in_dim(basis_full, place * share_rows, share_rows, 1)
        block = basis_full.astype(jnp.bfloat16)
    projected = jnp.dot(block, cusum, preferred_element_type=jnp.float32)
    return (basis_share, projected)


def solution(mesh):
    in_specs = (P("grp", "tm"), P())
    out_specs = (P(None, ("grp", "tm")), P(None, ("grp", "tm")))
    return jax.shard_map(body, mesh=mesh, in_specs=in_specs, out_specs=out_specs, check_vma=False)
```

profile of v0, /device:TPU:8, one launch (start us, length us, event | category | flops | bytes accessed | tf_op | source)
XLA Modules:
  0.0 462.1 jit_solution(2146260925044937070)
XLA Ops:
  7.2 11.6 %convolution_bitcast_fusion = f32[16384,256]{0,1:T(8,128)} fusion(bf16[16384,256]{1,0:T(8,128)(2,1)} %param.7), kind=kOutput, calls=%fused_computation.1 | convolution fusion | flops 2147614720 | bytes 25165824 | tf_op jit(solution)/shard_map/dot_general | solution.py:40
  18.8 1.7 slice.12
  20.6 38.3 %all-gather.3.cloned.1.call-done = f32[262144,1]{0,1:T(1,128)} async-done(((f32[16384,1]{0,1:T(1,128)}), f32[262144,1]{0,1:T(1,128)}) %all-gather.3.cloned.1.call-update) | async-done | bytes 1048592 | tf_op jit(solution)/shard_map/all_gather | solution.py:14
  58.8 0.6 broadcast.98
  59.4 10.4 %reduce.7 = f32[262144]{0:T(1024)S(1)} reduce(f32[262144,1]{0,1:T(1,128)} %all-gather.3.cloned.1.call-done, f32[]{:T(128)} %broadcast.98), dimensions={1}, to_apply=%all-gather.reduce_sub_computation.3 | reduce | bytes 2097156 | tf_op jit(solution)/shard_map/all_gather | solution.py:14
  69.8 0.2 reshape.30
  70.1 0.6 while.10
  70.1 0.1 constant_dynamic-slice_fusion.3
  70.3 0.1 constant_dynamic-slice_fusion.3
  70.4 0.1 constant_dynamic-slice_fusion.3
  70.5 0.1 constant_dynamic-slice_fusion.3
  70.7 86.4 %all-reduce.4.cloned.1.call-done = f32[16384]{0:T(1024)} async-done(((f32[16384]{0:T(1024)}), f32[16384]{0:T(1024)}) %all-reduce.4.cloned.1.call-update) | async-done | bytes 65552 | tf_op jit(solution)/shard_map/psum | solution.py:43
  157.1 13.3 %multiply_convert_fusion = bf16[16384,256]{0,1:T(8,128)(2,1)} fusion(f32[16384,256]{0,1:T(8,128)} %convolution_bitcast_fusion, f32[16384]{0:T(1024)} %all-reduce.4.cloned.1.call-done, f32[256]{0:T(256)S(1)} %get-tuple-element.45, f32[16384]{0:T(1024)S(1)} %get-tuple-element.27, f32[256]{0:T(256)S(1)} %get-tuple-element.44), kind=kLoop, calls=%fused_computation.3 | loop fusion | flops 41943040 | bytes 25298944 | tf_op jit(solution)/shard_map/convert_element_type | solution.py:53
  170.4 12.7 %fusion.3 = f32[32,16384]{1,0:T(8,128)} fusion(bf16[16384,256]{0,1:T(8,128)(2,1)} %multiply_convert_fusion, bf16[32,16384]{1,0:T(8,128)(2,1)S(1)} %copy-done), kind=kOutput, calls=%fused_computation.8 | convolution fusion | flops 536879104 | bytes 11534336 | tf_op jit(solution)/shard_map/dot_general | solution.py:59
  183.2 0.3 all-reduce.8.cloned.1.call-start
  183.4 96.8 %all-reduce.6.cloned.1.call-done = f32[32,16384]{1,0:T(8,128)} async-done(((f32[32,16384]{1,0:T(8,128)}), f32[32,16384]{1,0:T(8,128)}) %all-reduce.6.cloned.1.call-update) | async-done | bytes 2097168 | tf_op jit(solution)/shard_map/psum | solution.py:62
  280.3 4.7 %select_reduce_fusion.4 = (f32[]{:T(128)}, f32[32,32]{0,1:T(8,128)S(1)}) fusion(f32[32,16384]{1,0:T(8,128)} %all-reduce.6.cloned.1.call-done), kind=kOutput, calls=%fused_computation.53 | convolution fusion | flops 201329664 | bytes 2101252 | tf_op jit(solution)/shard_map/dot_general | solution.py:63
  285.6 0.1 copy.6
  285.7 2.9 cholesky.74
  288.7 0.6 compare_reduce_fusion.3
  289.3 0.7 fusion.8
  290.0 2.4 custom-call.8
  292.4 3.5 fusion.20
  295.9 2.4 select_reduce_fusion.3
  298.9 0.1 copy.9
  299.0 2.9 cholesky.85
  302.0 0.6 compare_reduce_fusion.2
  302.6 0.7 fusion.9
  303.3 2.4 custom-call.9
  305.7 2.9 convolution_convert_fusion
  308.6 13.3 %fusion.5 = f32[32,16384]{1,0:T(8,128)} fusion(bf16[16384,256]{0,1:T(8,128)(2,1)} %multiply_convert_fusion, bf16[32,16384]{1,0:T(8,128)(2,1)} %convolution_convert_fusion), kind=kOutput, calls=%fused_computation.11 | convolution fusion | flops 536879104 | bytes 11534336 | tf_op jit(solution)/shard_map/dot_general | solution.py:59
  322.0 97.3 %all-reduce.8.cloned.1.call-done = f32[32,16384]{1,0:T(8,128)} async-done(((f32[32,16384]{1,0:T(8,128)}), f32[32,16384]{1,0:T(8,128)}) %all-reduce.8.cloned.1.call-update) | async-done | bytes 2097168 | tf_op jit(solution)/shard_map/psum | solution.py:62
  419.2 4.6 %select_reduce_fusion.2 = (f32[]{:T(128)}, f32[32,32]{0,1:T(8,128)S(1)}) fusion(f32[32,16384]{1,0:T(8,128)} %all-reduce.8.cloned.1.call-done), kind=kOutput, calls=%fused_computation.49 | convolution fusion | flops 201329664 | bytes 2101252 | tf_op jit(solution)/shard_map/dot_general | solution.py:63
  424.5 0.1 copy.12
  424.6 2.9 cholesky.96
  427.6 0.6 compare_reduce_fusion.1
  428.2 0.7 fusion.10
  428.9 2.4 custom-call.10
  431.3 3.5 fusion.15
  434.8 2.4 select_reduce_fusion.1
  437.8 0.1 copy.15
  437.9 2.9 cholesky.107
  440.9 0.6 compare_reduce_fusion
  441.5 0.7 fusion.11
  442.2 2.4 custom-call.11
  444.6 1.9 fusion.12
  446.6 0.7 constant_dynamic-slice_fusion.1
  447.2 7.9 %fusion.1 = f32[32,256]{1,0:T(8,128)} fusion(f32[16384,256]{0,1:T(8,128)} %convolution_bitcast_fusion, f32[16384]{0:T(1024)S(1)} %copy-done.1, f32[256]{0:T(256)S(1)} %get-tuple-element.45, f32[16384]{0:T(1024)S(1)} %get-tuple-element.27, f32[256]{0:T(256)S(1)} %get-tuple-element.44, f32[32,16384]{1,0:T(8,128)S(1)} %fusion.12), kind=kOutput, calls=%fused_computation.6 | convolution fusion | flops 289931264 | bytes 19040256 | tf_op jit(solution)/shard_map/dot_general | solution.py:71
  (29 shorter events, 0.4 us)
Async XLA Ops:
  7.2 163.3 %copy-start = (bf16[32,16384]{1,0:T(8,128)(2,1)S(1)}, bf16[32,16384]{1,0:T(8,128)(2,1)}, u32[]{:S(2)}) copy-start(bf16[32,16384]{1,0:T(8,128)(2,1)} %param.8) | copy-start | bytes 3145732
  7.2 51.7 %all-gather.3.cloned.1.call-start = ((), (), s32[]{:S(2)}) async-start(), calls=%async_computation.3 | async-start | bytes 1114112 | tf_op jit(solution)/shard_map/all_gather | solution.py:14
  58.8 98.3 %all-reduce.4.cloned.1.call-start = ((), (), s32[]{:S(2)}) async-start(), calls=%async_computation | async-start | bytes 131072 | tf_op jit(solution)/shard_map/psum | solution.py:43
  70.1 210.2 %all-reduce.6.cloned.1.call-start = ((), (), s32[]{:S(2)}) async-start(), calls=%async_computation.1 | async-start | bytes 4194304 | tf_op jit(solution)/shard_map/psum | solution.py:62
  183.2 236.0 %all-reduce.8.cloned.1.call-start = ((), (), s32[]{:S(2)}) async-start(), calls=%async_computation.2 | async-start | bytes 4194304 | tf_op jit(solution)/shard_map/psum | solution.py:62
  321.9 125.3 %copy-start.1 = (f32[16384]{0:T(1024)S(1)}, f32[16384]{0:T(1024)}, u32[]{:S(2)}) copy-start(f32[16384]{0:T(1024)} %all-reduce.4.cloned.1.call-done) | copy-start | bytes 196612
Sparse Core Ops, SparseCore 0:
  20.7 38.1 all-gather.2
  70.2 86.8 all-reduce.3
  183.3 96.9 all-reduce.5
  322.1 97.1 all-reduce.7
where the time goes:
time: 469 us; the launch traced here: 462 us
  waiting for transfers between devices  319 us (68%)
  matrix products  71.4 us (15%)
  other arithmetic  50.6 us (11%)
  between operations  17 us (4%)
    psum x2, waiting for transfers between devices, body(): image = lax.psum(local_image, 'tm')  194 us
    psum x1, waiting for transfers between devices, body(): total = lax.psum(own_total, 'tm')  86.4 us
    all_gather x1, waiting for transfers between devices, prefix_2(): gathered = lax.all_gather(part, axis)  38.3 us
    dot_general x2, matrix products, body(): lax.dot_general(scores, sparse, (((1,), (1,)), ((), ())), preferred_eleme...  26.1 us
    convert_element_type x1, other arithmetic, body(): (jnp.sign(raw) * jnp.maximum(jnp.abs(raw) - THRESH, 0.0)).astype(jnp.bflo...  13.3 us
    dot_general x1, matrix products, body(): partial_sums = jnp.dot(series, triangle, preferred_element_type=jnp.float32)  11.6 us
    all_gather x1, other arithmetic, prefix_2(): gathered = lax.all_gather(part, axis)  10.4 us
  transfers between devices with their start and end apart: 4, of which 4 were waited for; matrix products, arithmetic and copies ran while one was open for 0% of the time, Pallas kernels for 0%

commit v1 on v0

v1 whole, which is shorter than its diff:
```python
import functools

import jax
import jax.numpy as jnp
from jax import lax
from jax.experimental import pallas as pl
from jax.experimental.pallas import tpu as pltpu
from jax.sharding import PartitionSpec as P

ITERS = 2
THRESH = 1.0
LANES = 128
SUB = 8
MESH = pl.DeviceIdType.MESH
HIGHEST = lax.Precision.HIGHEST
NT = (((1,), (1,)), ((), ()))


def remote(src, dst, send_sem, recv_sem, peer):
    return pltpu.make_async_remote_copy(
        src_ref=src, dst_ref=dst, send_sem=send_sem, recv_sem=recv_sem,
        device_id={"tm": peer}, device_id_type=MESH,
    )


def inverse_factor(gram):
    width = gram.shape[0]
    rows = lax.broadcasted_iota(jnp.int32, (width, LANES), 0)
    cols = lax.broadcasted_iota(jnp.int32, (width, LANES), 1)
    eye = (rows == cols).astype(jnp.float32)
    trace = jnp.sum(jnp.sum(gram * eye, axis=1, keepdims=True), axis=0, keepdims=True)
    amount = 1e-05 * trace / width + 1e-06
    work = gram + amount * eye + (cols == rows + width).astype(jnp.float32)
    pivots = jnp.zeros((width, 1), jnp.float32)
    for j in range(width):
        top = work[j : j + 1, :]
        pivot = top[:, j : j + 1]
        column = work[:, j : j + 1]
        below = lax.broadcasted_iota(jnp.int32, (width, 1), 0)
        factor = jnp.where(below > j, column / pivot, 0.0)
        pivots = jnp.where(below == j, pivot, pivots)
        work = work - factor * top
    inverse = pltpu.roll(work, LANES - width, 1) * lax.rsqrt(pivots)
    return inverse[:, :width]


def kernel(n, series_ref, start_ref, tri_ref, corr_ref, weight_ref, basis_ref, proj_ref,
           sparse, cusum, lhs, tot_send, tot_recv, bt_send, bt_recv,
           one_send, one_recv, two_send, two_recv, gram_send, gram_recv, blk,
           tot_ss, tot_rs, bt_ss, bt_rs, one_ss, one_rs, two_ss, two_rs,
           gram_ss, gram_rs, ag_ss, ag_rs, fw_ss, fw_rs):
    total_rows, steps = series_ref.shape
    vectors = start_ref.shape[0]
    share = total_rows // n
    tiles = share // LANES
    half = n // 2
    me = lax.axis_index("tm")
    core = me % 2
    chip = me // 2
    partner = me + 1 - 2 * core

    barrier = pltpu.get_barrier_semaphore()

    @pl.loop(1, n)
    def _(i):
        pl.semaphore_signal(barrier, inc=1, device_id={"tm": (me + i) % n}, device_id_type=MESH)

    ones = jnp.ones((SUB, steps), jnp.bfloat16)
    row8 = lax.broadcasted_iota(jnp.int32, (SUB, LANES), 0)

    @pl.loop(0, n)
    def _(p):
        part = series_ref[pl.ds(pl.multiple_of(p * share, share), share), :]
        sums = lax.dot_general(ones, part, NT, preferred_element_type=jnp.float32)
        tile = jnp.zeros((SUB, LANES), jnp.float32)
        for q in range(tiles):
            tile = jnp.where(row8 == q, sums[:, q * LANES : (q + 1) * LANES], tile)
        tot_send[p] = tile

    pl.semaphore_wait(barrier, n - 1)

    def tot_copy(i):
        p = (me + i) % n
        return remote(tot_send.at[p], tot_recv.at[me], tot_ss.at[p], tot_rs.at[me], p)

    def tot_from(i):
        p = (me + i) % n
        return remote(tot_send.at[p], tot_recv.at[p], tot_ss.at[p], tot_rs.at[p], p)

    pl.loop(1, n)(lambda i: tot_copy(i).start())
    tot_recv[me] = tot_send[me]
    pl.loop(1, n)(lambda i: tot_from(i).wait_recv())

    def running(d, state):
        bt_send[d, 0] = state
        return state + tot_recv[d]

    total = lax.fori_loop(0, n, running, jnp.zeros((SUB, LANES), jnp.float32))

    def bt_copy(i):
        p = (me + i) % n
        return remote(bt_send.at[p], bt_recv.at[me], bt_ss.at[p], bt_rs.at[me], p)

    def bt_from(p):
        return remote(bt_send.at[p], bt_recv.at[p], bt_ss.at[p], bt_rs.at[p], p)

    @pl.loop(1, n)
    def _(i):
        bt_send[(me + i) % n, 1] = total
        bt_copy(i).start()

    bt_send[me, 1] = total
    bt_recv[me] = bt_send[me]

    def pieces(value):
        high = value.astype(jnp.bfloat16).astype(jnp.float32)
        rest = value - high
        mid = rest.astype(jnp.bfloat16).astype(jnp.float32)
        return [high, mid, rest - mid]

    weight = weight_ref[0:1, :]

    @pl.loop(0, n)
    def _(i):
        p = (me + i) % n

        @pl.when(i > 0)
        def _():
            bt_from(p).wait_recv()

        both = bt_recv[p]
        before, whole = pieces(both[0]), pieces(both[1])
        zero = jnp.zeros((SUB, LANES), jnp.float32)
        stack = jnp.concatenate(before + whole + whole + [zero] * 7, axis=0)
        lhs[...] = stack.T.astype(jnp.bfloat16)

        for q in range(tiles):
            rows = pl.ds(pl.multiple_of(p * share + q * LANES, LANES), LANES)
            prefix = jnp.dot(series_ref[rows, :], tri_ref[...], preferred_element_type=jnp.float32)
            prefix += jnp.dot(lhs[...], corr_ref[q], preferred_element_type=jnp.float32)
            raw = weight * prefix
            cusum[rows, :] = raw.astype(jnp.bfloat16)
            soft = raw - jnp.clip(raw, -THRESH, THRESH)
            sparse[rows, :] = soft.astype(jnp.bfloat16)

    def share_of(p):
        return pl.ds(pl.multiple_of(p * share, share), share)

    lane32 = lax.broadcasted_iota(jnp.int32, (vectors, LANES), 1)

    def sum_gram(k, value):
        part = lax.dot_general(value, value, NT, precision=HIGHEST, preferred_element_type=jnp.float32)
        wide = jnp.concatenate([part] * (LANES // vectors), axis=1)
        packed = jnp.zeros((SUB, LANES), jnp.float32)
        lane8 = lax.broadcasted_iota(jnp.int32, (SUB, LANES), 1) // vectors
        for g in range(vectors // SUB):
            packed = jnp.where(lane8 == g, wide[g * SUB : (g + 1) * SUB, :], packed)
        gram_send[k] = packed

        def out(i):
            p = (me + i) % n
            return remote(gram_send.at[k], gram_recv.at[k, me], gram_ss.at[k, p], gram_rs.at[k, me], p)

        def into(i):
            p = (me + i) % n
            return remote(gram_send.at[k], gram_recv.at[k, p], gram_ss.at[k, p], gram_rs.at[k, p], p)

        pl.loop(1, n)(lambda i: out(i).start())
        gram_recv[k, me] = packed
        pl.loop(1, n)(lambda i: into(i).wait_recv())
        full = lax.fori_loop(0, n, lambda d, s: s + gram_recv[k, d], jnp.zeros((SUB, LANES), jnp.float32))
        pl.loop(1, n)(lambda i: out(i).wait_send())
        parts = [full] + [pltpu.roll(full, LANES - g * vectors, 1) for g in range(1, vectors // SUB)]
        return jnp.where(lane32 < vectors, jnp.concatenate(parts, axis=0), 0.0)

    def gathered_dot(step, target):
        def ag_in(i):
            c = (chip + i) % half
            o = 2 * c + core
            return remote(blk.at[step, o], blk.at[step, o], ag_ss.at[step, c], ag_rs.at[step, c], o)

        def fw_out(i):
            c = (chip + i) % half
            o = 2 * c + core
            return remote(blk.at[step, o], blk.at[step, o], fw_ss.at[step, c], fw_rs.at[step, c], partner)

        def fw_in(i):
            c = (chip + i) % half
            o = 2 * c + 1 - core
            return remote(blk.at[step, o], blk.at[step, o], fw_ss.at[step, c], fw_rs.at[step, c], partner)

        def one(i, acc):
            c = (chip + i) % half

            @pl.when(i > 0)
            def _():
                ag_in(i).wait_recv()

            fw_out(i).start()
            o = 2 * c + core
            return acc + jnp.dot(blk[step, o], target[share_of(o), :], preferred_element_type=jnp.float32)

        def other(i, acc):
            c = (chip + i) % half
            fw_in(i).wait_recv()
            o = 2 * c + 1 - core
            return acc + jnp.dot(blk[step, o], target[share_of(o), :], preferred_element_type=jnp.float32)

        acc = lax.fori_loop(0, half, one, jnp.zeros((vectors, steps), jnp.float32))
        acc = lax.fori_loop(0, half, other, acc)
        pl.loop(0, half)(lambda i: fw_out(i).wait_send())
        return acc

    for step in range(ITERS):
        if step == 0:
            def first_scores(p, acc):
                return acc + jnp.dot(
                    start_ref[:, share_of(p)], sparse[share_of(p), :], preferred_element_type=jnp.float32
                )

            scores = lax.fori_loop(0, n, first_scores, jnp.zeros((vectors, steps), jnp.float32))
        else:
            scores = gathered_dot(step - 1, sparse)
        scores = scores.astype(jnp.bfloat16)

        def image_of(p):
            return lax.dot_general(scores, sparse[share_of(p), :], NT, preferred_element_type=jnp.float32)

        def one_copy(i):
            c = (chip + 1 + i) % half
            return remote(one_send.at[c], one_recv.at[step, c], one_ss.at[step, c], one_rs.at[step, c], partner)

        def two_copy(i):
            c = (chip + 1 + i) % half
            return remote(two_send.at[c], two_recv.at[step, chip], two_ss.at[step, c], two_rs.at[step, chip],
                          2 * c + core)

        def two_from(i):
            c = (chip + 1 + i) % half
            return remote(two_send.at[c], two_recv.at[step, c], two_ss.at[step, c], two_rs.at[step, c],
                          2 * c + core)

        @pl.loop(0, half)
        def _(i):
            c = (chip + 1 + i) % half
            one_send[c] = image_of(2 * c + 1 - core)
            one_copy(i).start()

        @pl.loop(0, half - 1)
        def _(i):
            c = (chip + 1 + i) % half
            own = image_of(2 * c + core)
            one_copy(i).wait_recv()
            two_send[c] = own + one_recv[step, c]
            two_copy(i).start()

        own = image_of(2 * chip + core)
        one_copy(half - 1).wait_recv()
        two_send[chip] = own + one_recv[step, chip]

        def add(i, acc):
            c = (chip + 1 + i) % half
            two_from(i).wait_recv()
            return acc + two_recv[step, c]

        image = lax.fori_loop(0, half - 1, add, two_send[chip])
        pl.loop(0, half)(lambda i: one_copy(i).wait_send())
        pl.loop(0, half - 1)(lambda i: two_copy(i).wait_send())

        inverse = inverse_factor(sum_gram(2 * step, image))
        first = jnp.dot(inverse, image, precision=HIGHEST, preferred_element_type=jnp.float32)
        inverse = inverse_factor(sum_gram(2 * step + 1, first))
        basis = jnp.dot(inverse, first, precision=HIGHEST, preferred_element_type=jnp.float32)
        blk[step, me] = basis.astype(jnp.bfloat16)

        def ag_copy(i):
            c = (chip + i) % half
            return remote(blk.at[step, me], blk.at[step, me], ag_ss.at[step, c], ag_rs.at[step, chip],
                          2 * c + core)

        pl.loop(1, half)(lambda i: ag_copy(i).start())
        if step == ITERS - 1:
            basis_ref[...] = basis
            proj_ref[...] = gathered_dot(step, cusum)
            pl.loop(1, half)(lambda i: ag_copy(i).wait_send())
        else:
            pl.loop(1, half)(lambda i: ag_copy(i).wait_send())

    pl.loop(1, n)(lambda i: tot_copy(i).wait_send())
    pl.loop(1, n)(lambda i: bt_copy(i).wait_send())


def body(series, start_block):
    series_count, blocks = series.shape
    vectors = start_block.shape[0]
    n = lax.axis_size("tm")
    place = lax.axis_index("tm")
    share = series_count // n
    tiles = share // LANES
    half = n // 2
    row_id = lax.broadcasted_iota(jnp.int32, (blocks, blocks), 0)
    col_id = lax.broadcasted_iota(jnp.int32, (blocks, blocks), 1)
    triangle = (row_id <= col_id).astype(jnp.bfloat16)
    steps_f = jnp.float32(blocks * n)
    t_local = (place * blocks + jnp.arange(1, blocks + 1, dtype=jnp.int32)).astype(jnp.float32)
    weight = jnp.where(
        t_local < steps_f, jnp.sqrt(steps_f / jnp.maximum(t_local * (steps_f - t_local), 1.0)), 0.0
    )
    coarse = (place * blocks).astype(jnp.float32) / steps_f
    coarse = jnp.full((blocks,), 1.0, jnp.float32) * coarse
    fine = jnp.arange(1, blocks + 1, dtype=jnp.int32).astype(jnp.float32) / steps_f
    one = jnp.ones((blocks,), jnp.float32)
    none = jnp.zeros((blocks,), jnp.float32)
    kinds = jnp.stack([one] * 3 + [-coarse] * 3 + [-fine] * 3 + [none] * 7)
    pick = jnp.eye(SUB, dtype=jnp.float32)[:tiles]
    corr = (pick[:, None, :, None] * kinds[None, :, None, :]).reshape(tiles, LANES, blocks)
    corr = corr.astype(jnp.bfloat16)
    weight8 = jnp.broadcast_to(weight[None, :], (SUB, blocks))

    f32, bf16 = jnp.float32, jnp.bfloat16
    vmem = pl.BlockSpec(memory_space=pltpu.VMEM)
    dma = pltpu.SemaphoreType.DMA
    return pl.pallas_call(
        functools.partial(kernel, n),
        out_shape=(
            jax.ShapeDtypeStruct((vectors, share), f32),
            jax.ShapeDtypeStruct((vectors, blocks), f32),
        ),
        in_specs=[vmem] * 5,
        out_specs=(vmem, vmem),
        scratch_shapes=[
            pltpu.VMEM((series_count, blocks), bf16),
            pltpu.VMEM((series_count, blocks), bf16),
            pltpu.VMEM((LANES, LANES), bf16),
            pltpu.VMEM((n, SUB, LANES), f32),
            pltpu.VMEM((n, SUB, LANES), f32),
            pltpu.VMEM((n, 2, SUB, LANES), f32),
            pltpu.VMEM((n, 2, SUB, LANES), f32),
            pltpu.VMEM((half, vectors, share), f32),
            pltpu.VMEM((ITERS, half, vectors, share), f32),
            pltpu.VMEM((half, vectors, share), f32),
            pltpu.VMEM((ITERS, half, vectors, share), f32),
            pltpu.VMEM((2 * ITERS, SUB, LANES), f32),
            pltpu.VMEM((2 * ITERS, n, SUB, LANES), f32),
            pltpu.VMEM((ITERS, n, vectors, share), bf16),
            dma((n,)), dma((n,)), dma((n,)), dma((n,)),
            dma((ITERS, half)), dma((ITERS, half)), dma((ITERS, half)), dma((ITERS, half)),
            dma((2 * ITERS, n)), dma((2 * ITERS, n)),
            dma((ITERS, half)), dma((ITERS, half)), dma((ITERS, half)), dma((ITERS, half)),
        ],
        compiler_params=pltpu.CompilerParams(
            collective_id=0, has_side_effects=True, vmem_limit_bytes=56 * 1024 * 1024
        ),
        cost_estimate=pl.CostEstimate(
            flops=2 * series_count * blocks * (blocks + 6 * vectors), bytes_accessed=series_count * blocks * 2,
            transcendentals=0,
        ),
    )(series, start_block, triangle, corr, weight8)


def solution(mesh):
    in_specs = (P("grp", "tm"), P())
    out_specs = (P(None, ("grp", "tm")), P(None, ("grp", "tm")))
    return jax.shard_map(body, mesh=mesh, in_specs=in_specs, out_specs=out_specs, check_vma=False)
```

time: 469 us -> 159 us (0.34); the launches traced: 462 us -> 158 us
  waiting for transfers between devices: 319 us -> 0 us
  Pallas kernels: 0 us -> 152 us
  matrix products: 71.4 us -> 0 us
  other arithmetic: 50.6 us -> 1.69 us
  between operations: 17 us -> 0.71 us
    psum x3 -> x0, waiting for transfers between devices: 280 us -> none  [the longest x2 194 us: body(): image = lax.psum(local_image, 'tm')]
    pallas_call x0 -> x1, Pallas kernels: none -> 152 us  [body(): pl.pallas_call(functools.partial(kernel, n), out_shape=(jax.ShapeDtypeStr...]
    dot_general x8 -> x0, matrix products: 59.6 us -> none  [the longest x2 26.1 us: body(): lax.dot_general(scores, sparse, (((1,), (1,)), ((), ())), preferred_eleme...]
    all_gather x1 -> x0, waiting for transfers between devices: 38.3 us -> none  [prefix_2(): gathered = lax.all_gather(part, axis)]
    another operation x20 -> x0, other arithmetic: 26.7 us -> none  [the longest x6 7.18 us: body(): lower = jnp.linalg.cholesky(shifted(gram))]
    another operation x4 -> x0, matrix products: 11.8 us -> none  [the longest x2 6.98 us: body(): first = jax.scipy.linalg.solve_triangular(lower, image, lower=True)]
    convert_element_type x1 -> x3, other arithmetic: 13.3 us -> 1.67 us  [the longest x1 0.99 us: body(): corr = corr.astype(jnp.bfloat16)]
    all_gather x1 -> x0, other arithmetic: 10.4 us -> none  [prefix_2(): gathered = lax.all_gather(part, axis)]
  transfers between devices with their start and end apart: 4 -> 0, of which waited for: 4 -> 0; matrix products, arithmetic and copies ran while one was open for 0% -> 0% of each run, Pallas kernels for 0% -> 0%
where the time goes in v1:
time: 159 us; the launch traced here: 158 us
  Pallas kernels  152 us (96%)
  local copies, waits for them, and re-layouts  3.72 us (2%)
  other arithmetic  1.69 us (1%)
    pallas_call x1, Pallas kernels, body(): pl.pallas_call(functools.partial(kernel, n), out_shape=(jax.ShapeDtypeStr...  152 us

profile of v1, /device:TPU:8, one launch (start us, length us, event | category | flops | bytes accessed | tf_op | source)
XLA Modules:
  0.0 158.0 jit_solution(16294638598727651545)
XLA Ops:
  0.7 0.1 stack.24
  0.8 0.6 broadcast_in_dim.4.weight_ref
  1.4 0.1 mul.35
  1.5 0.7 fusion.tri_ref
  2.2 1.0 multiply_convert_fusion.corr_ref
  3.2 151.9 %shard_map.41 = (f32[32,1024]{1,0:T(8,128)}, f32[32,256]{1,0:T(8,128)}) custom-call(bf16[16384,256]{1,0:T(8,128)(2,1)} %series_ref.1, bf16[32,16384]{1,0:T(8,128)(2,1)} %start_ref.1, bf16[256,256]{1,0:T(8,128)(2,1)} %fusion.tri_ref, bf16[8,128,256]{2,1,0:T(8,128)(2,1)} %multiply_convert_fusion.corr_ref, f32[8,256]{1,0:T(8,128)} %broadcast_in_dim.4.weight_ref), custom_call_target="tpu_custom_call" | custom-call | flops 3758096384 | bytes 8388608 | tf_op jit(solution)/shard_map/pallas_call | solution.py:323
  155.0 1.6 copy.6
  156.6 1.4 copy.7
  (11 shorter events, 0.1 us)

commit v2 on v1

--- a/solution.py
+++ b/solution.py
@@ -44,11 +44,11 @@
     return inverse[:, :width]
 
 
-def kernel(n, series_ref, start_ref, tri_ref, corr_ref, weight_ref, basis_ref, proj_ref,
-           sparse, cusum, lhs, tot_send, tot_recv, bt_send, bt_recv,
-           one_send, one_recv, two_send, two_recv, gram_send, gram_recv, blk,
-           tot_ss, tot_rs, bt_ss, bt_rs, one_ss, one_rs, two_ss, two_rs,
-           gram_ss, gram_rs, ag_ss, ag_rs, fw_ss, fw_rs):
+def kernel(n, inner, series_ref, start_ref, basis_ref, proj_ref,
+           sparse, cusum, lhs, tri_ref, corr_ref, tot_send, tot_recv, bt_send, bt_recv,
+           one_send, one_recv, near_send, near_recv, far_send, far_recv, gram_send, gram_recv, blk,
+           tot_ss, tot_rs, bt_ss, bt_rs, one_ss, one_rs, near_ss, near_rs,
+           far_ss, far_rs, gram_ss, gram_rs, ag_ss, ag_rs, row_ss, row_rs, fw_ss, fw_rs):
     total_rows, steps = series_ref.shape
     vectors = start_ref.shape[0]
     share = total_rows // n
@@ -58,12 +58,35 @@
     core = me % 2
     chip = me // 2
     partner = me + 1 - 2 * core
+    outer = half // inner
+    near = chip % inner
+    far = chip // inner
+
+    def device(a, b, side):
+        return 2 * (a * inner + b) + side
 
     barrier = pltpu.get_barrier_semaphore()
 
     @pl.loop(1, n)
     def _(i):
         pl.semaphore_signal(barrier, inc=1, device_id={"tm": (me + i) % n}, device_id_type=MESH)
+
+    steps_f = jnp.float32(steps * n)
+    tri_rows = lax.broadcasted_iota(jnp.int32, (steps, steps), 0)
+    tri_cols = lax.broadcasted_iota(jnp.int32, (steps, steps), 1)
+    tri_ref[...] = (tri_rows <= tri_cols).astype(jnp.float32).astype(jnp.bfloat16)
+    step_id = lax.broadcasted_iota(jnp.int32, (1, steps), 1) + 1
+    t_local = (me * steps + step_id).astype(jnp.float32)
+    weight = jnp.where(
+        t_local < steps_f, jnp.sqrt(steps_f / jnp.maximum(t_local * (steps_f - t_local), 1.0)), 0.0
+    )
+    coarse = -(jnp.zeros((1, steps), jnp.int32) + me * steps).astype(jnp.float32) / steps_f
+    fine = -step_id.astype(jnp.float32) / steps_f
+    kind = lax.broadcasted_iota(jnp.int32, (LANES, steps), 0)
+    values = jnp.where(kind < 3 * SUB, 1.0, jnp.where(kind < 6 * SUB, coarse, fine))
+    for q in range(tiles):
+        used = (kind % SUB == q) & (kind < 9 * SUB)
+        corr_ref[q] = jnp.where(used, values, 0.0).astype(jnp.bfloat16)
 
     ones = jnp.ones((SUB, steps), jnp.bfloat16)
     row8 = lax.broadcasted_iota(jnp.int32, (SUB, LANES), 0)
@@ -118,8 +141,6 @@
         mid = rest.astype(jnp.bfloat16).astype(jnp.float32)
         return [high, mid, rest - mid]
 
-    weight = weight_ref[0:1, :]
-
     @pl.loop(0, n)
     def _(i):
         p = (me + i) % n
@@ -174,41 +195,67 @@
         return jnp.where(lane32 < vectors, jnp.concatenate(parts, axis=0), 0.0)
 
     def gathered_dot(step, target):
+        def along(i):
+            return (far + i) % outer
+
+        def across(k):
+            return (near + k) % inner
+
         def ag_in(i):
-            c = (chip + i) % half
-            o = 2 * c + core
-            return remote(blk.at[step, o], blk.at[step, o], ag_ss.at[step, c], ag_rs.at[step, c], o)
-
-        def fw_out(i):
-            c = (chip + i) % half
-            o = 2 * c + core
-            return remote(blk.at[step, o], blk.at[step, o], fw_ss.at[step, c], fw_rs.at[step, c], partner)
-
-        def fw_in(i):
-            c = (chip + i) % half
-            o = 2 * c + 1 - core
-            return remote(blk.at[step, o], blk.at[step, o], fw_ss.at[step, c], fw_rs.at[step, c], partner)
+            o = device(along(i), near, core)
+            return remote(blk.at[step, o], blk.at[step, o], ag_ss.at[step, along(i)], ag_rs.at[step, along(i)], o)
+
+        def row_out(i, k):
+            o = device(along(i), near, core)
+            return remote(blk.at[step, o], blk.at[step, o], row_ss.at[step, along(i), across(k)],
+                          row_rs.at[step, along(i), near], device(far, across(k), core))
+
+        def row_in(i, k):
+            o = device(along(i), across(k), core)
+            return remote(blk.at[step, o], blk.at[step, o], row_ss.at[step, along(i), across(k)],
+                          row_rs.at[step, along(i), across(k)], device(far, across(k), core))
+
+        def forward(i, k, side):
+            a, b = along(i), across(k)
+            o = device(a, b, side)
+            return remote(blk.at[step, o], blk.at[step, o], fw_ss.at[step, a, b], fw_rs.at[step, a, b], partner)
+
+        def add(acc, o):
+            return acc + jnp.dot(blk[step, o], target[share_of(o), :], preferred_element_type=jnp.float32)
 
         def one(i, acc):
-            c = (chip + i) % half
-
             @pl.when(i > 0)
             def _():
                 ag_in(i).wait_recv()
 
-            fw_out(i).start()
-            o = 2 * c + core
-            return acc + jnp.dot(blk[step, o], target[share_of(o), :], preferred_element_type=jnp.float32)
+            pl.loop(1, inner)(lambda k: row_out(i, k).start())
+            forward(i, 0, core).start()
+            return add(acc, device(along(i), near, core))
+
+        def two(i, acc):
+            def inner_two(k, acc):
+                row_in(i, k).wait_recv()
+                forward(i, k, core).start()
+                return add(acc, device(along(i), across(k), core))
+
+            return lax.fori_loop(1, inner, inner_two, acc)
 
         def other(i, acc):
-            c = (chip + i) % half
-            fw_in(i).wait_recv()
-            o = 2 * c + 1 - core
-            return acc + jnp.dot(blk[step, o], target[share_of(o), :], preferred_element_type=jnp.float32)
-
-        acc = lax.fori_loop(0, half, one, jnp.zeros((vectors, steps), jnp.float32))
-        acc = lax.fori_loop(0, half, other, acc)
-        pl.loop(0, half)(lambda i: fw_out(i).wait_send())
+            def inner_other(k, acc):
+                forward(i, k, 1 - core).wait_recv()
+                return add(acc, device(along(i), across(k), 1 - core))
+
+            return lax.fori_loop(0, inner, inner_other, acc)
+
+        acc = lax.fori_loop(0, outer, one, jnp.zeros((vectors, steps), jnp.float32))
+        acc = lax.fori_loop(0, outer, two, acc)
+        acc = lax.fori_loop(0, outer, other, acc)
+
+        @pl.loop(0, outer)
+        def _(i):
+            pl.loop(1, inner)(lambda k: row_out(i, k).wait_send())
+            pl.loop(0, inner)(lambda k: forward(i, k, core).wait_send())
+
         return acc
 
     for step in range(ITERS):
@@ -226,46 +273,82 @@
         def image_of(p):
             return lax.dot_general(scores, sparse[share_of(p), :], NT, preferred_element_type=jnp.float32)
 
-        def one_copy(i):
-            c = (chip + 1 + i) % half
-            return remote(one_send.at[c], one_recv.at[step, c], one_ss.at[step, c], one_rs.at[step, c], partner)
-
-        def two_copy(i):
-            c = (chip + 1 + i) % half
-            return remote(two_send.at[c], two_recv.at[step, chip], two_ss.at[step, c], two_rs.at[step, chip],
-                          2 * c + core)
-
-        def two_from(i):
-            c = (chip + 1 + i) % half
-            return remote(two_send.at[c], two_recv.at[step, c], two_ss.at[step, c], two_rs.at[step, c],
-                          2 * c + core)
-
-        @pl.loop(0, half)
+        def along(i):
+            return (far + 1 + i) % outer
+
+        def across(k):
+            return (near + k) % inner
+
+        def one_copy(i, k):
+            a, b = along(i), across(k)
+            return remote(one_send.at[a, b], one_recv.at[step, a, b], one_ss.at[step, a, b],
+                          one_rs.at[step, a, b], partner)
+
+        def near_copy(i, k):
+            a, b = along(i), across(k)
+            return remote(near_send.at[a, b], near_recv.at[step, a, near], near_ss.at[step, a, b],
+                          near_rs.at[step, a, near], device(far, b, core))
+
+        def near_from(i, k):
+            a, b = along(i), across(k)
+            return remote(near_send.at[a, b], near_recv.at[step, a, b], near_ss.at[step, a, b],
+                          near_rs.at[step, a, b], device(far, b, core))
+
+        def far_copy(i):
+            a = along(i)
+            return remote(far_send.at[a], far_recv.at[step, far], far_ss.at[step, a], far_rs.at[step, far],
+                          device(a, near, core))
+
+        def far_from(i):
+            a = along(i)
+            return remote(far_send.at[a], far_recv.at[step, a], far_ss.at[step, a], far_rs.at[step, a],
+                          device(a, near, core))
+
+        @pl.loop(0, outer)
         def _(i):
-            c = (chip + 1 + i) % half
-            one_send[c] = image_of(2 * c + 1 - core)
-            one_copy(i).start()
-
-        @pl.loop(0, half - 1)
+            @pl.loop(0, inner)
+            def _(j):
+                k = (j + 1) % inner
+                one_send[along(i), across(k)] = image_of(device(along(i), across(k), 1 - core))
+                one_copy(i, k).start()
+
+        @pl.loop(0, outer)
         def _(i):
-            c = (chip + 1 + i) % half
-            own = image_of(2 * c + core)
-            one_copy(i).wait_recv()
-            two_send[c] = own + one_recv[step, c]
-            two_copy(i).start()
-
-        own = image_of(2 * chip + core)
-        one_copy(half - 1).wait_recv()
-        two_send[chip] = own + one_recv[step, chip]
+            @pl.loop(1, inner)
+            def _(k):
+                own = image_of(device(along(i), across(k), core))
+                one_copy(i, k).wait_recv()
+                near_send[along(i), across(k)] = own + one_recv[step, along(i), across(k)]
+                near_copy(i, k).start()
+
+            own = image_of(device(along(i), near, core))
+            one_copy(i, 0).wait_recv()
+            far_send[along(i)] = own + one_recv[step, along(i), near]
+
+        def gather_near(i):
+            def add(k, acc):
+                near_from(i, k).wait_recv()
+                return acc + near_recv[step, along(i), across(k)]
+
+            return lax.fori_loop(1, inner, add, far_send[along(i)])
+
+        @pl.loop(0, outer - 1)
+        def _(i):
+            far_send[along(i)] = gather_near(i)
+            far_copy(i).start()
 
         def add(i, acc):
-            c = (chip + 1 + i) % half
-            two_from(i).wait_recv()
-            return acc + two_recv[step, c]
-
-        image = lax.fori_loop(0, half - 1, add, two_send[chip])
-        pl.loop(0, half)(lambda i: one_copy(i).wait_send())
-        pl.loop(0, half - 1)(lambda i: two_copy(i).wait_send())
+            far_from(i).wait_recv()
+            return acc + far_recv[step, along(i)]
+
+        image = lax.fori_loop(0, outer - 1, add, gather_near(outer - 1))
+
+        @pl.loop(0, outer)
+        def _(i):
+            pl.loop(0, inner)(lambda k: one_copy(i, k).wait_send())
+            pl.loop(1, inner)(lambda k: near_copy(i, k).wait_send())
+
+        pl.loop(0, outer - 1)(lambda i: far_copy(i).wait_send())
 
         inverse = inverse_factor(sum_gram(2 * step, image))
         first = jnp.dot(inverse, image, precision=HIGHEST, preferred_element_type=jnp.float32)
@@ -274,17 +357,17 @@
         blk[step, me] = basis.astype(jnp.bfloat16)
 
         def ag_copy(i):
-            c = (chip + i) % half
-            return remote(blk.at[step, me], blk.at[step, me], ag_ss.at[step, c], ag_rs.at[step, chip],
-                          2 * c + core)
-
-        pl.loop(1, half)(lambda i: ag_copy(i).start())
+            a = (far + i) % outer
+            return remote(blk.at[step, me], blk.at[step, me], ag_ss.at[step, a], ag_rs.at[step, far],
+                          device(a, near, core))
+
+        pl.loop(1, outer)(lambda i: ag_copy(i).start())
         if step == ITERS - 1:
             basis_ref[...] = basis
             proj_ref[...] = gathered_dot(step, cusum)
-            pl.loop(1, half)(lambda i: ag_copy(i).wait_send())
+            pl.loop(1, outer)(lambda i: ag_copy(i).wait_send())
         else:
-            pl.loop(1, half)(lambda i: ag_copy(i).wait_send())
+            pl.loop(1, outer)(lambda i: ag_copy(i).wait_send())
 
     pl.loop(1, n)(lambda i: tot_copy(i).wait_send())
     pl.loop(1, n)(lambda i: bt_copy(i).wait_send())
@@ -294,59 +377,52 @@
     series_count, blocks = series.shape
     vectors = start_block.shape[0]
     n = lax.axis_size("tm")
-    place = lax.axis_index("tm")
     share = series_count // n
     tiles = share // LANES
     half = n // 2
-    row_id = lax.broadcasted_iota(jnp.int32, (blocks, blocks), 0)
-    col_id = lax.broadcasted_iota(jnp.int32, (blocks, blocks), 1)
-    triangle = (row_id <= col_id).astype(jnp.bfloat16)
-    steps_f = jnp.float32(blocks * n)
-    t_local = (place * blocks + jnp.arange(1, blocks + 1, dtype=jnp.int32)).astype(jnp.float32)
-    weight = jnp.where(
-        t_local < steps_f, jnp.sqrt(steps_f / jnp.maximum(t_local * (steps_f - t_local), 1.0)), 0.0
-    )
-    coarse = (place * blocks).astype(jnp.float32) / steps_f
-    coarse = jnp.full((blocks,), 1.0, jnp.float32) * coarse
-    fine = jnp.arange(1, blocks + 1, dtype=jnp.int32).astype(jnp.float32) / steps_f
-    one = jnp.ones((blocks,), jnp.float32)
-    none = jnp.zeros((blocks,), jnp.float32)
-    kinds = jnp.stack([one] * 3 + [-coarse] * 3 + [-fine] * 3 + [none] * 7)
-    pick = jnp.eye(SUB, dtype=jnp.float32)[:tiles]
-    corr = (pick[:, None, :, None] * kinds[None, :, None, :]).reshape(tiles, LANES, blocks)
-    corr = corr.astype(jnp.bfloat16)
-    weight8 = jnp.broadcast_to(weight[None, :], (SUB, blocks))
+    inner = 1
+    while 4 * inner * inner <= half:
+        inner *= 2
+    outer = half // inner
 
     f32, bf16 = jnp.float32, jnp.bfloat16
     vmem = pl.BlockSpec(memory_space=pltpu.VMEM)
     dma = pltpu.SemaphoreType.DMA
     return pl.pallas_call(
-        functools.partial(kernel, n),
+        functools.partial(kernel, n, inner),
         out_shape=(
             jax.ShapeDtypeStruct((vectors, share), f32),
             jax.ShapeDtypeStruct((vectors, blocks), f32),
         ),
-        in_specs=[vmem] * 5,
+        in_specs=[vmem] * 2,
         out_specs=(vmem, vmem),
         scratch_shapes=[
             pltpu.VMEM((series_count, blocks), bf16),
             pltpu.VMEM((series_count, blocks), bf16),
             pltpu.VMEM((LANES, LANES), bf16),
+            pltpu.VMEM((blocks, blocks), bf16),
+            pltpu.VMEM((tiles, LANES, blocks), bf16),
             pltpu.VMEM((n, SUB, LANES), f32),
             pltpu.VMEM((n, SUB, LANES), f32),
             pltpu.VMEM((n, 2, SUB, LANES), f32),
             pltpu.VMEM((n, 2, SUB, LANES), f32),
-            pltpu.VMEM((half, vectors, share), f32),
-            pltpu.VMEM((ITERS, half, vectors, share), f32),
-            pltpu.VMEM((half, vectors, share), f32),
-            pltpu.VMEM((ITERS, half, vectors, share), f32),
+            pltpu.VMEM((outer, inner, vectors, share), f32),
+            pltpu.VMEM((ITERS, outer, inner, vectors, share), f32),
+            pltpu.VMEM((outer, inner, vectors, share), f32),
+            pltpu.VMEM((ITERS, outer, inner, vectors, share), f32),
+            pltpu.VMEM((outer, vectors, share), f32),
+            pltpu.VMEM((ITERS, outer, vectors, share), f32),
             pltpu.VMEM((2 * ITERS, SUB, LANES), f32),
             pltpu.VMEM((2 * ITERS, n, SUB, LANES), f32),
             pltpu.VMEM((ITERS, n, vectors, share), bf16),
             dma((n,)), dma((n,)), dma((n,)), dma((n,)),
-            dma((ITERS, half)), dma((ITERS, half)), dma((ITERS, half)), dma((ITERS, half)),
+            dma((ITERS, outer, inner)), dma((ITERS, outer, inner)),
+            dma((ITERS, outer, inner)), dma((ITERS, outer, inner)),
+            dma((ITERS, outer)), dma((ITERS, outer)),
             dma((2 * ITERS, n)), dma((2 * ITERS, n)),
-            dma((ITERS, half)), dma((ITERS, half)), dma((ITERS, half)), dma((ITERS, half)),
+            dma((ITERS, outer)), dma((ITERS, outer)),
+            dma((ITERS, outer, inner)), dma((ITERS, outer, inner)),
+            dma((ITERS, outer, inner)), dma((ITERS, outer, inner)),
         ],
         compiler_params=pltpu.CompilerParams(
             collective_id=0, has_side_effects=True, vmem_limit_bytes=56 * 1024 * 1024
@@ -355,7 +431,7 @@
             flops=2 * series_count * blocks * (blocks + 6 * vectors), bytes_accessed=series_count * blocks * 2,
             transcendentals=0,
         ),
-    )(series, start_block, triangle, corr, weight8)
+    )(series, start_block)
 
 
 def solution(mesh):

time: 159 us -> 141 us (0.89)
  Pallas kernels: 152 us -> 137 us
  other arithmetic: 1.69 us -> 0 us
    pallas_call x1, Pallas kernels: 152 us -> 137 us  [body(): pl.pallas_call(functools.partial(kernel, n, inner), out_shape=(jax.ShapeD...]
    convert_element_type x3 -> x0, other arithmetic: 1.67 us -> none  [the longest x1 0.99 us: body(): corr = corr.astype(jnp.bfloat16)]
where the time goes in v2:
time: 141 us; the launch traced here: 140 us
  Pallas kernels  137 us (97%)
  local copies, waits for them, and re-layouts  2.94 us (2%)
    pallas_call x1, Pallas kernels, body(): pl.pallas_call(functools.partial(kernel, n, inner), out_shape=(jax.ShapeD...  137 us
    unnamed x2, local copies, waits for them, and re-layouts  2.94 us

profile of v2, /device:TPU:8, one launch (start us, length us, event | category | flops | bytes accessed | tf_op | source)
XLA Modules:
  0.0 140.3 jit_solution(15269829724797446373)
XLA Ops:
  0.6 136.7 %shard_map.41 = (f32[32,1024]{1,0:T(8,128)}, f32[32,256]{1,0:T(8,128)}) custom-call(bf16[16384,256]{1,0:T(8,128)(2,1)} %series_ref.1, bf16[32,16384]{1,0:T(8,128)(2,1)} %start_ref.1), custom_call_target="tpu_custom_call" | custom-call | flops 3758096384 | bytes 8388608 | tf_op jit(solution)/shard_map/pallas_call | solution.py:391
  137.4 1.6 %copy.6 = f32[32,1024]{1,0:T(8,128)} copy(f32[32,1024]{1,0:T(8,128)} %get-tuple-element.4) | data formatting | bytes 262144
  138.9 1.4 copy.7

commit v3 on v2

--- a/solution.py
+++ b/solution.py
@@ -21,6 +21,14 @@
         src_ref=src, dst_ref=dst, send_sem=send_sem, recv_sem=recv_sem,
         device_id={"tm": peer}, device_id_type=MESH,
     )
+
+
+def each(low, high, run):
+    if high - low <= 16:
+        for i in range(low, high):
+            run(i)
+    else:
+        pl.loop(low, high)(run)
 
 
 def inverse_factor(gram):
@@ -44,12 +52,12 @@
     return inverse[:, :width]
 
 
-def kernel(n, inner, series_ref, start_ref, basis_ref, proj_ref,
-           sparse, cusum, lhs, tri_ref, corr_ref, tot_send, tot_recv, bt_send, bt_recv,
+def kernel(n, inner, series_hbm, start_hbm, basis_ref, proj_ref,
+           series_ref, start_ref, load_sem, sparse, cusum, lhs, tri_ref, corr_ref, tot_send, tot_recv, bt_send, bt_recv,
            one_send, one_recv, near_send, near_recv, far_send, far_recv, gram_send, gram_recv, blk,
            tot_ss, tot_rs, bt_ss, bt_rs, one_ss, one_rs, near_ss, near_rs,
            far_ss, far_rs, gram_ss, gram_rs, ag_ss, ag_rs, row_ss, row_rs, fw_ss, fw_rs):
-    total_rows, steps = series_ref.shape
+    total_rows, steps = series_hbm.shape
     vectors = start_ref.shape[0]
     share = total_rows // n
     tiles = share // LANES
@@ -64,6 +72,14 @@
 
     def device(a, b, side):
         return 2 * (a * inner + b) + side
+
+    def load(p):
+        rows = pl.ds(pl.multiple_of(p * share, share), share)
+        return pltpu.make_async_copy(series_hbm.at[rows, :], series_ref.at[rows, :], load_sem.at[p])
+
+    load_start = pltpu.make_async_copy(start_hbm, start_ref, load_sem.at[n])
+    each(0, n, lambda p: load(p).start())
+    load_start.start()
 
     barrier = pltpu.get_barrier_semaphore()
 
@@ -93,6 +109,7 @@
 
     @pl.loop(0, n)
     def _(p):
+        load(p).wait()
         part = series_ref[pl.ds(pl.multiple_of(p * share, share), share), :]
         sums = lax.dot_general(ones, part, NT, preferred_element_type=jnp.float32)
         tile = jnp.zeros((SUB, LANES), jnp.float32)
@@ -110,9 +127,9 @@
         p = (me + i) % n
         return remote(tot_send.at[p], tot_recv.at[p], tot_ss.at[p], tot_rs.at[p], p)
 
-    pl.loop(1, n)(lambda i: tot_copy(i).start())
+    each(1, n, lambda i: tot_copy(i).start())
     tot_recv[me] = tot_send[me]
-    pl.loop(1, n)(lambda i: tot_from(i).wait_recv())
+    each(1, n, lambda i: tot_from(i).wait_recv())
 
     def running(d, state):
         bt_send[d, 0] = state
@@ -127,10 +144,11 @@
     def bt_from(p):
         return remote(bt_send.at[p], bt_recv.at[p], bt_ss.at[p], bt_rs.at[p], p)
 
-    @pl.loop(1, n)
-    def _(i):
+    def send_back(i):
         bt_send[(me + i) % n, 1] = total
         bt_copy(i).start()
+
+    each(1, n, send_back)
 
     bt_send[me, 1] = total
     bt_recv[me] = bt_send[me]
@@ -141,8 +159,9 @@
         mid = rest.astype(jnp.bfloat16).astype(jnp.float32)
         return [high, mid, rest - mid]
 
-    @pl.loop(0, n)
-    def _(i):
+    load_start.wait()
+
+    def transform(i, acc):
         p = (me + i) % n
 
         @pl.when(i > 0)
@@ -162,11 +181,17 @@
             raw = weight * prefix
             cusum[rows, :] = raw.astype(jnp.bfloat16)
             soft = raw - jnp.clip(raw, -THRESH, THRESH)
-            sparse[rows, :] = soft.astype(jnp.bfloat16)
+            soft = soft.astype(jnp.bfloat16)
+            sparse[rows, :] = soft
+        return acc
+
+    lax.fori_loop(0, n, transform, 0)
 
     def share_of(p):
         return pl.ds(pl.multiple_of(p * share, share), share)
 
+    late = []
+    sent = []
     lane32 = lax.broadcasted_iota(jnp.int32, (vectors, LANES), 1)
 
     def sum_gram(k, value):
@@ -186,11 +211,11 @@
             p = (me + i) % n
             return remote(gram_send.at[k], gram_recv.at[k, p], gram_ss.at[k, p], gram_rs.at[k, p], p)
 
-        pl.loop(1, n)(lambda i: out(i).start())
+        each(1, n, lambda i: out(i).start())
         gram_recv[k, me] = packed
-        pl.loop(1, n)(lambda i: into(i).wait_recv())
-        full = lax.fori_loop(0, n, lambda d, s: s + gram_recv[k, d], jnp.zeros((SUB, LANES), jnp.float32))
-        pl.loop(1, n)(lambda i: out(i).wait_send())
+        each(1, n, lambda i: into(i).wait_recv())
+        full = jnp.sum(gram_recv[k], axis=0)
+        late.append(lambda: each(1, n, lambda i: out(i).wait_send()))
         parts = [full] + [pltpu.roll(full, LANES - g * vectors, 1) for g in range(1, vectors // SUB)]
         return jnp.where(lane32 < vectors, jnp.concatenate(parts, axis=0), 0.0)
 
@@ -228,7 +253,7 @@
             def _():
                 ag_in(i).wait_recv()
 
-            pl.loop(1, inner)(lambda k: row_out(i, k).start())
+            each(1, inner, lambda k: row_out(i, k).start())
             forward(i, 0, core).start()
             return add(acc, device(along(i), near, core))
 
@@ -251,11 +276,13 @@
         acc = lax.fori_loop(0, outer, two, acc)
         acc = lax.fori_loop(0, outer, other, acc)
 
-        @pl.loop(0, outer)
-        def _(i):
-            pl.loop(1, inner)(lambda k: row_out(i, k).wait_send())
-            pl.loop(0, inner)(lambda k: forward(i, k, core).wait_send())
-
+        def finish():
+            @pl.loop(0, outer)
+            def _(i):
+                each(1, inner, lambda k: row_out(i, k).wait_send())
+                each(0, inner, lambda k: forward(i, k, core).wait_send())
+
+        late.append(finish)
         return acc
 
     for step in range(ITERS):
@@ -279,12 +306,12 @@
         def across(k):
             return (near + k) % inner
 
-        def one_copy(i, k):
+        def one_copy(i, k, step=step):
             a, b = along(i), across(k)
             return remote(one_send.at[a, b], one_recv.at[step, a, b], one_ss.at[step, a, b],
                           one_rs.at[step, a, b], partner)
 
-        def near_copy(i, k):
+        def near_copy(i, k, step=step):
             a, b = along(i), across(k)
             return remote(near_send.at[a, b], near_recv.at[step, a, near], near_ss.at[step, a, b],
                           near_rs.at[step, a, near], device(far, b, core))
@@ -294,7 +321,7 @@
             return remote(near_send.at[a, b], near_recv.at[step, a, b], near_ss.at[step, a, b],
                           near_rs.at[step, a, b], device(far, b, core))
 
-        def far_copy(i):
+        def far_copy(i, step=step):
             a = along(i)
             return remote(far_send.at[a], far_recv.at[step, far], far_ss.at[step, a], far_rs.at[step, far],
                           device(a, near, core))
@@ -303,6 +330,10 @@
             a = along(i)
             return remote(far_send.at[a], far_recv.at[step, a], far_ss.at[step, a], far_rs.at[step, a],
                           device(a, near, core))
+
+        for done in sent:
+            done()
+        sent.clear()
 
         @pl.loop(0, outer)
         def _(i):
@@ -343,12 +374,15 @@
 
         image = lax.fori_loop(0, outer - 1, add, gather_near(outer - 1))
 
-        @pl.loop(0, outer)
-        def _(i):
-            pl.loop(0, inner)(lambda k: one_copy(i, k).wait_send())
-            pl.loop(1, inner)(lambda k: near_copy(i, k).wait_send())
-
-        pl.loop(0, outer - 1)(lambda i: far_copy(i).wait_send())
+        def finish(one_copy=one_copy, near_copy=near_copy, far_copy=far_copy):
+            @pl.loop(0, outer)
+            def _(i):
+                each(0, inner, lambda k: one_copy(i, k).wait_send())
+                each(1, inner, lambda k: near_copy(i, k).wait_send())
+
+            each(0, outer - 1, lambda i: far_copy(i).wait_send())
+
+        sent.append(finish)
 
         inverse = inverse_factor(sum_gram(2 * step, image))
         first = jnp.dot(inverse, image, precision=HIGHEST, preferred_element_type=jnp.float32)
@@ -356,21 +390,21 @@
         basis = jnp.dot(inverse, first, precision=HIGHEST, preferred_element_type=jnp.float32)
         blk[step, me] = basis.astype(jnp.bfloat16)
 
-        def ag_copy(i):
+        def ag_copy(i, step=step):
             a = (far + i) % outer
             return remote(blk.at[step, me], blk.at[step, me], ag_ss.at[step, a], ag_rs.at[step, far],
                           device(a, near, core))
 
-        pl.loop(1, outer)(lambda i: ag_copy(i).start())
+        each(1, outer, lambda i: ag_copy(i).start())
+        late.append(lambda ag_copy=ag_copy: each(1, outer, lambda i: ag_copy(i).wait_send()))
         if step == ITERS - 1:
             basis_ref[...] = basis
             proj_ref[...] = gathered_dot(step, cusum)
-            pl.loop(1, outer)(lambda i: ag_copy(i).wait_send())
-        else:
-            pl.loop(1, outer)(lambda i: ag_copy(i).wait_send())
-
-    pl.loop(1, n)(lambda i: tot_copy(i).wait_send())
-    pl.loop(1, n)(lambda i: bt_copy(i).wait_send())
+
+    for done in sent + late:
+        done()
+    each(1, n, lambda i: tot_copy(i).wait_send())
+    each(1, n, lambda i: bt_copy(i).wait_send())
 
 
 def body(series, start_block):
@@ -388,15 +422,19 @@
     f32, bf16 = jnp.float32, jnp.bfloat16
     vmem = pl.BlockSpec(memory_space=pltpu.VMEM)
     dma = pltpu.SemaphoreType.DMA
+    hbm = pl.BlockSpec(memory_space=pl.ANY)
     return pl.pallas_call(
         functools.partial(kernel, n, inner),
         out_shape=(
             jax.ShapeDtypeStruct((vectors, share), f32),
             jax.ShapeDtypeStruct((vectors, blocks), f32),
         ),
-        in_specs=[vmem] * 2,
+        in_specs=[hbm] * 2,
         out_specs=(vmem, vmem),
         scratch_shapes=[
+            pltpu.VMEM((series_count, blocks), bf16),
+            pltpu.VMEM((vectors, series_count), bf16),
+            dma((n + 1,)),
             pltpu.VMEM((series_count, blocks), bf16),
             pltpu.VMEM((series_count, blocks), bf16),
             pltpu.VMEM((LANES, LANES), bf16),

time: 141 us -> 136 us (0.965)
  Pallas kernels: 137 us -> 132 us
    pallas_call x1, Pallas kernels: 137 us -> 132 us  [body(): pl.pallas_call(functools.partial(kernel, n, inner), out_shape=(jax.ShapeD...]
where the time goes in v3:
time: 136 us
  Pallas kernels  132 us (97%)
  local copies, waits for them, and re-layouts  2.94 us (2%)
    pallas_call x1, Pallas kernels, body(): pl.pallas_call(functools.partial(kernel, n, inner), out_shape=(jax.ShapeD...  132 us
    unnamed x2, local copies, waits for them, and re-layouts  2.94 us

profile of v3, /device:TPU:8, one launch (start us, length us, event | category | flops | bytes accessed | tf_op | source)
XLA Modules:
  0.0 135.7 jit_solution(10064334126626723063)
XLA Ops:
  0.6 132.1 %shard_map.41 = (f32[32,1024]{1,0:T(8,128)}, f32[32,256]{1,0:T(8,128)}) custom-call(bf16[16384,256]{1,0:T(8,128)(2,1)} %series_hbm.1, bf16[32,16384]{1,0:T(8,128)(2,1)} %start_hbm.1), custom_call_target="tpu_custom_call" | custom-call | flops 3758096384 | bytes 8388608 | tf_op jit(solution)/shard_map/pallas_call | solution.py:426
  132.8 1.6 %copy.6 = f32[32,1024]{1,0:T(8,128)} copy(f32[32,1024]{1,0:T(8,128)} %get-tuple-element.4) | data formatting | bytes 262144
  134.3 1.4 %copy.7 = f32[32,256]{1,0:T(8,128)} copy(f32[32,256]{1,0:T(8,128)} %get-tuple-element.5) | data formatting | bytes 65536

commit v4 on v3

--- a/solution.py
+++ b/solution.py
@@ -335,26 +335,33 @@
             done()
         sent.clear()
 
+        def give(i, k):
+            one_send[along(i), across(k)] = image_of(device(along(i), across(k), 1 - core))
+            one_copy(i, k).start()
+
+        def keep(i, k):
+            own = image_of(device(along(i), across(k), core))
+            one_copy(i, k).wait_recv()
+            return own + one_recv[step, along(i), across(k)]
+
+        pl.loop(1, inner)(lambda k: give(0, k))
+
         @pl.loop(0, outer)
         def _(i):
-            @pl.loop(0, inner)
-            def _(j):
-                k = (j + 1) % inner
-                one_send[along(i), across(k)] = image_of(device(along(i), across(k), 1 - core))
-                one_copy(i, k).start()
+            @pl.when(i < outer - 1)
+            def _():
+                pl.loop(1, inner)(lambda k: give(i + 1, k))
+
+            @pl.loop(1, inner)
+            def _(k):
+                near_send[along(i), across(k)] = keep(i, k)
+                near_copy(i, k).start()
+
+        pl.loop(0, outer)(lambda i: give(i, 0))
 
         @pl.loop(0, outer)
         def _(i):
-            @pl.loop(1, inner)
-            def _(k):
-                own = image_of(device(along(i), across(k), core))
-                one_copy(i, k).wait_recv()
-                near_send[along(i), across(k)] = own + one_recv[step, along(i), across(k)]
-                near_copy(i, k).start()
-
-            own = image_of(device(along(i), near, core))
-            one_copy(i, 0).wait_recv()
-            far_send[along(i)] = own + one_recv[step, along(i), near]
+            far_send[along(i)] = keep(i, 0)
 
         def gather_near(i):
             def add(k, acc):

time: 136 us -> 135 us (level)
  no operation moved by 1% of the time
where the time goes in v4:
time: 135 us
  Pallas kernels  131 us (97%)
  local copies, waits for them, and re-layouts  2.94 us (2%)
    pallas_call x1, Pallas kernels, body(): pl.pallas_call(functools.partial(kernel, n, inner), out_shape=(jax.ShapeD...  131 us
    unnamed x2, local copies, waits for them, and re-layouts  2.94 us

profile of v4, /device:TPU:8, one launch (start us, length us, event | category | flops | bytes accessed | tf_op | source)
XLA Modules:
  0.0 134.8 jit_solution(2611339160059188801)
XLA Ops:
  0.6 131.2 %shard_map.41 = (f32[32,1024]{1,0:T(8,128)}, f32[32,256]{1,0:T(8,128)}) custom-call(bf16[16384,256]{1,0:T(8,128)(2,1)} %series_hbm.1, bf16[32,16384]{1,0:T(8,128)(2,1)} %start_hbm.1), custom_call_target="tpu_custom_call" | custom-call | flops 3758096384 | bytes 8388608 | tf_op jit(solution)/shard_map/pallas_call | solution.py:433
  131.8 1.6 %copy.6 = f32[32,1024]{1,0:T(8,128)} copy(f32[32,1024]{1,0:T(8,128)} %get-tuple-element.4) | data formatting | bytes 262144
  133.4 1.4 %copy.7 = f32[32,256]{1,0:T(8,128)} copy(f32[32,256]{1,0:T(8,128)} %get-tuple-element.5) | data formatting | bytes 65536

commit v5 on v4

--- a/solution.py
+++ b/solution.py
@@ -29,6 +29,14 @@
             run(i)
     else:
         pl.loop(low, high)(run)
+
+
+def fold(low, high, run, state):
+    if high - low <= 16:
+        for i in range(low, high):
+            state = run(i, state)
+        return state
+    return lax.fori_loop(low, high, run, state)
 
 
 def inverse_factor(gram):
@@ -135,7 +143,7 @@
         bt_send[d, 0] = state
         return state + tot_recv[d]
 
-    total = lax.fori_loop(0, n, running, jnp.zeros((SUB, LANES), jnp.float32))
+    total = fold(0, n, running, jnp.zeros((SUB, LANES), jnp.float32))
 
     def bt_copy(i):
         p = (me + i) % n
@@ -292,7 +300,7 @@
                     start_ref[:, share_of(p)], sparse[share_of(p), :], preferred_element_type=jnp.float32
                 )
 
-            scores = lax.fori_loop(0, n, first_scores, jnp.zeros((vectors, steps), jnp.float32))
+            scores = fold(0, n, first_scores, jnp.zeros((vectors, steps), jnp.float32))
         else:
             scores = gathered_dot(step - 1, sparse)
         scores = scores.astype(jnp.bfloat16)
@@ -357,7 +365,7 @@
                 near_send[along(i), across(k)] = keep(i, k)
                 near_copy(i, k).start()
 
-        pl.loop(0, outer)(lambda i: give(i, 0))
+        each(0, outer, lambda i: give(i, 0))
 
         @pl.loop(0, outer)
         def _(i):

time: 135 us -> 133 us (0.985)
    pallas_call x1, Pallas kernels: 131 us -> 130 us  [body(): pl.pallas_call(functools.partial(kernel, n, inner), out_shape=(jax.ShapeD...]
where the time goes in v5:
time: 133 us
  Pallas kernels  130 us (98%)
  local copies, waits for them, and re-layouts  2.94 us (2%)
    pallas_call x1, Pallas kernels, body(): pl.pallas_call(functools.partial(kernel, n, inner), out_shape=(jax.ShapeD...  130 us
    unnamed x2, local copies, waits for them, and re-layouts  2.94 us

profile of v5, /device:TPU:8, one launch (start us, length us, event | category | flops | bytes accessed | tf_op | source)
XLA Modules:
  0.0 133.1 jit_solution(3567883997816840801)
XLA Ops:
  0.6 129.6 %shard_map.41 = (f32[32,1024]{1,0:T(8,128)}, f32[32,256]{1,0:T(8,128)}) custom-call(bf16[16384,256]{1,0:T(8,128)(2,1)} %series_hbm.1, bf16[32,16384]{1,0:T(8,128)(2,1)} %start_hbm.1), custom_call_target="tpu_custom_call" | custom-call | flops 3758096384 | bytes 8388608 | tf_op jit(solution)/shard_map/pallas_call | solution.py:441
  130.2 1.6 %copy.6 = f32[32,1024]{1,0:T(8,128)} copy(f32[32,1024]{1,0:T(8,128)} %get-tuple-element.4) | data formatting | bytes 262144
  131.8 1.4 %copy.7 = f32[32,256]{1,0:T(8,128)} copy(f32[32,256]{1,0:T(8,128)} %get-tuple-element.5) | data formatting | bytes 65536
